TPU v7x, 128 devices: a whole 4x4x4 slice. The times are simulated.
128 devices in a mesh: ctx: 16 (over z_hi, x, core), tp: 8 (over y, z_lo).
Axes of the slice: x: 4, y: 4, z: 4 (z_hi: 2, z_lo: 2; z = z_hi * 2 + z_lo), core: 2. Of those that a mesh axis runs over, the one named last changes fastest.
Arguments:
- hidden_in: bfloat16 [4096, 4096], P('ctx', 'tp'), may hold values from -6 to 6
- upstream: bfloat16 [4096, 4096], P('ctx', 'tp'), may hold values from -6 to 6
- query_ckpt: bfloat16 [4096, 4096], P('ctx', 'tp'), may hold values from -110 to 110
- keyval_ckpt: bfloat16 [4096, 2048], P('ctx', 'tp'), may hold values from -5.5 to 5.5
- attn_out_grad: bfloat16 [4096, 4096], P('ctx', 'tp'), may hold values from -6 to 6
- segments: int32 [4096], replicated, may hold values from 0 to 1, never falling along the last dimension, each value on 1 to 3072 neighbouring positions
- query_weight: bfloat16 [4096, 4096], P(None, 'tp'), may hold values from -0.09375 to 0.09375
- keyval_weight: bfloat16 [4096, 2048], P(None, 'tp'), may hold values from -0.125 to 0.125
- mix_weight: bfloat16 [4096, 8192], P(None, 'tp'), may hold values from -0.0625 to 0.0625
- out_weight: bfloat16 [8192, 4096], P('tp'), may hold values from -0.09375 to 0.09375
- state_in_ckpt: bfloat16 [4096, 1024], P('ctx', 'tp'), may hold values from -3 to 3
- state_out_ckpt: bfloat16 [4096, 1024], P('ctx', 'tp'), may hold values from -3 to 3
- step_size: float32 [4096, 128], P('ctx', 'tp'), may hold values from 0.004 to 0.04
- decay_rate: float32 [128], P('tp'), may hold values from 0.02 to 20
- skip_gain: float32 [128], P('tp'), may hold values from 0.5 to 1.5
Outputs:
- grad_mid: bfloat16 [4096, 4096], P('ctx', 'tp')
- grad_hidden: bfloat16 [4096, 4096], P('ctx', 'tp')
- grad_state_in: float32 [4096, 1024], P('ctx', 'tp')
Inputs may be any that keep to these rules, and one draw needn't show every extreme that they name: `segments`: document ids never fall along the sequence; every document has 1 to 3072 tokens.
All inputs are finite; a program needn't handle non-finite values.
Results may differ from a plain program's by a relative error of at most 0.02.
Values may be sent and summed in bfloat16 or wider, within the bound.
A program may use at most 192 MiB of HBM per device.

v0:
```python
import jax
import jax.numpy as jnp
from jax import lax
from jax.experimental import pallas as pl
from jax.experimental.pallas import tpu as pltpu
from jax.sharding import PartitionSpec as P

HIGH = lax.Precision.HIGHEST
MESH = pl.DeviceIdType.MESH
VM = pl.BlockSpec(memory_space=pltpu.VMEM)
F32 = jnp.float32
BF16 = jnp.bfloat16


def remote(src, dst, send, recv, to):
    return pltpu.make_async_remote_copy(
        src_ref=src, dst_ref=dst, send_sem=send, recv_sem=recv, device_id=to, device_id_type=MESH
    )


def greet(peers):
    barrier = pltpu.get_barrier_semaphore()
    for peer in peers:
        pl.semaphore_signal(barrier, inc=1, device_id=peer, device_id_type=MESH)
    pl.semaphore_wait(barrier, len(peers))


def params(cid, mib=40):
    return pltpu.CompilerParams(
        collective_id=cid, has_side_effects=True, vmem_limit_bytes=mib << 20
    )


def tp_places():
    c = lax.axis_index("ctx")
    me = lax.axis_index("tp")
    zp = me + 1 - 2 * lax.rem(me, 2)
    return c, me, zp, lax.rem(me + 2, 8), lax.rem(me + 6, 8)


def ctx_places():
    tp = lax.axis_index("tp")
    me = lax.axis_index("ctx")
    core = lax.rem(me, 2)
    x = lax.rem(me // 2, 4)
    zh = me // 8

    def at(z, place, c):
        return z * 8 + lax.rem(place, 4) * 2 + c

    return tp, me, core, x, zh, at


def dot(left, right, over, precision=None):
    return lax.dot_general(
        left,
        right,
        (((over[0],), (over[1],)), ((), ())),
        preferred_element_type=F32,
        precision=precision,
    )


def lower(n):
    row = lax.broadcasted_iota(jnp.int32, (n, n), 0)
    col = lax.broadcasted_iota(jnp.int32, (n, n), 1)
    return (col <= row).astype(F32)


def sent_sums(term, add, buf, base, ssem, rsem, beside):
    c, me, zp, up, down = tp_places()
    opp = lax.rem(me + 4, 8)

    def other(k):
        return k + 1 - 2 * lax.rem(k, 2)

    tin, uin, win, vin, out = buf
    half = tin.shape[0] // 2
    lo, hi = pl.ds(0, half), pl.ds(half, half)
    copies = []

    def cp(k, src, dst, to):
        copy = remote(src, dst, ssem.at[base + k], rsem.at[base + k], (c, to))
        copy.start()
        copies.append(copy)
        return copy

    out[0] = term(other(opp)).astype(BF16)
    a = [cp(n, out.at[0, part], tin.at[part], zp) for n, part in enumerate((lo, hi))]
    out[1] = term(other(up)).astype(BF16)
    w0 = [cp(2, out.at[1, lo], win.at[0, lo], up)]
    out[2] = term(other(down)).astype(BF16)
    w1 = [cp(3, out.at[2, lo], win.at[1, lo], down)]
    w0.append(cp(4, out.at[1, hi], win.at[0, hi], up))
    w1.append(cp(5, out.at[2, hi], win.at[1, hi], down))
    to_up = term(up)
    out[5, hi] = to_up[half:].astype(BF16)
    to_down = term(down)
    out[6, lo] = to_down[:half].astype(BF16)
    held = term(opp)
    a[0].wait_recv()
    out[3, lo] = (held[:half] + tin[lo].astype(F32)).astype(BF16)
    t0 = cp(6, out.at[3, lo], uin.at[0], up)
    u0 = [cp(8, out.at[5, hi], win.at[2, hi], up)]
    u1 = [cp(9, out.at[6, lo], win.at[3, lo], down)]
    a[1].wait_recv()
    out[3, hi] = (held[half:] + tin[hi].astype(F32)).astype(BF16)
    t1 = cp(7, out.at[3, hi], uin.at[1], down)
    held = term(zp)
    v = []
    for n, part in enumerate((lo, hi)):
        w0[n].wait_recv()
        w1[n].wait_recv()
        rows = slice(n * half, (n + 1) * half)
        out[4, part] = (
            held[rows] + win[0, part].astype(F32) + win[1, part].astype(F32)
        ).astype(BF16)
        v.append(cp(10 + n, out.at[4, part], vin.at[part], zp))
    t0.wait_recv()
    out[5, lo] = (to_up[:half] + uin[0].astype(F32)).astype(BF16)
    u0.append(cp(12, out.at[5, lo], win.at[2, lo], up))
    t1.wait_recv()
    out[6, hi] = (to_down[half:] + uin[1].astype(F32)).astype(BF16)
    u1.append(cp(13, out.at[6, hi], win.at[3, hi], down))
    held = term(me) + add()
    beside()
    for copy in v + u0 + u1:
        copy.wait_recv()
    result = held + vin[...].astype(F32) + win[2].astype(F32) + win[3].astype(F32)
    for copy in copies:
        copy.wait_send()
    return result


def spread_out(mine, everyone, base, ssem, rsem, use):
    c, me, zp, up, down = tp_places()
    opp = lax.rem(me + 4, 8)

    def other(k):
        return k + 1 - 2 * lax.rem(k, 2)

    half = everyone.shape[1] // 2
    lo, hi = pl.ds(0, half), pl.ds(half, half)
    copies = []

    def cp(k, slot, to, part=None):
        ref = everyone.at[slot] if part is None else everyone.at[slot, part]
        copy = remote(ref, ref, ssem.at[base + k], rsem.at[base + k], (c, to))
        copy.start()
        copies.append(copy)
        return copy

    everyone[me] = mine
    c1 = [cp(0, me, up, lo)]
    c2 = [cp(1, me, down, hi)]
    c0 = [cp(2, me, zp, lo)]
    c1.append(cp(3, me, up, hi))
    c2.append(cp(4, me, down, lo))
    c0.append(cp(5, me, zp, hi))
    use(me)
    c1[0].wait_recv()
    c5 = cp(6, down, up, lo)
    c2[0].wait_recv()
    c6 = cp(7, up, down, hi)
    c0[0].wait_recv()
    late = [cp(8, zp, up, lo), cp(9, zp, down, lo)]
    c0[1].wait_recv()
    late += [cp(10, zp, up, hi), cp(11, zp, down, hi)]
    use(zp)
    c5.wait_recv()
    c7 = cp(12, opp, zp, lo)
    c1[1].wait_recv()
    use(down)
    c6.wait_recv()
    c8 = cp(13, opp, zp, hi)
    c2[1].wait_recv()
    use(up)
    use(opp)
    for copy in late:
        copy.wait_recv()
    use(other(down))
    use(other(up))
    c7.wait_recv()
    c8.wait_recv()
    use(other(opp))
    for copy in copies:
        copy.wait_send()


def prefix_weights(logs, heads):
    tp, me, core, x, zh, at = ctx_places()
    j = lax.broadcasted_iota(jnp.int32, (16, 128), 0)
    jz, jx, jc = j // 8, lax.rem(j // 2, 4), lax.rem(j, 2)

    def factor(mask, scale):
        log = dot(logs, jnp.where(mask, 1.0, 0.0), (0, 0), HIGH)
        return jnp.exp(log) * scale

    one = jnp.float32(1.0)
    zero = jnp.float32(0.0)
    same = (jz == zh) & (jx == x)
    rows = [
        factor(same & (jc + 1 == core), one),
        factor(same & (jc + core == 0), one),
    ]
    for d in range(4):
        rows.append(factor((jz == zh) & (jx < lax.rem(x + d, 4)), one))
    for d in range(4):
        to = lax.rem(x + d, 4)
        rows.append(
            factor((jz == zh) & (jx > x) & (jx < to), jnp.where(to > x, one, zero))
        )
    rows.append(factor((jz == 0) & (jx > x), jnp.where(zh == 0, one, zero)))
    rows.append(factor(same & (jc == core + 1), one))
    rows.append(jnp.full((heads, 128), jnp.where(core == 0, one, zero)))
    return rows


def whole_kernel(
    kv_hbm, q_hbm, g_hbm, hid_hbm, qw_hbm, kw_hbm, ow_hbm, mw_hbm, up_hbm, b_hbm, c_hbm,
    step_ref, decay_ref, seg_ref, skip_ref,
    mid_ref, hidden_ref, state_ref,
    kv, kvall, s_ref, q4, g4, top, t4, d4, p,
    got, uin, vin, zin, tout, uout, zout, dq_ref, kvg_ref, hid, cum_ref, cumt_ref, steps, logs,
    qw, kw, ow, mw, up_ref, b_ref, c_ref, tin, tuin, rin, rv, rout, everyone, y_acc, y, mixed,
    local, w_ref, terms, ours_out, theirs, gx, hout, hin, eout, ein, carried,
    ssem, rsem, hssem, hrsem, tssem, trsem, lsem,
):
    tp, me, core, x, zh, at = ctx_places()
    c, tme, tzp, tup, tdown = tp_places()
    topp = lax.rem(tme + 4, 8)
    mate = at(zh, x, 1 - core)
    right, left, opp = at(zh, x + 1, core), at(zh, x + 3, core), at(zh, x + 2, core)
    zp = at(1 - zh, x, core)
    heads, rows, size = q4.shape
    scaling = size ** (-0.5)
    own_rows = pl.ds(0, rows)
    loads = [pltpu.make_async_copy(kv_hbm, kv.at[own_rows], lsem.at[0])]
    hid_own = pltpu.make_async_copy(hid_hbm, hid.at[tme], lsem.at[1])
    weights = [
        pltpu.make_async_copy(src, dst, lsem.at[2 + k])
        for k, (src, dst) in enumerate(((qw_hbm, qw), (kw_hbm, kw), (ow_hbm, ow), (mw_hbm, mw)))
    ]
    more = [
        pltpu.make_async_copy(src, dst, lsem.at[6 + k])
        for k, (src, dst) in enumerate(((up_hbm, up_ref), (b_hbm, b_ref), (c_hbm, c_ref)))
    ]
    for h in range(heads):
        lanes = pl.ds(h * size, size)
        loads.append(pltpu.make_async_copy(q_hbm.at[:, lanes], q4.at[h], lsem.at[9 + h]))
        loads.append(pltpu.make_async_copy(g_hbm.at[:, lanes], g4.at[h], lsem.at[9 + heads + h]))
    loads[0].start()
    hid_own.start()
    for load in loads[1:] + weights + more:
        load.start()
    barrier = pltpu.get_barrier_semaphore()
    peers = [(c, tzp), (c, tup), (c, tdown), (mate, tp), (right, tp), (left, tp), (zp, tp)]
    for peer in peers:
        pl.semaphore_signal(barrier, inc=1, device_id=peer, device_id_type=MESH)

    groups = step_ref.shape[0]
    tri = lower(rows)
    eye = jnp.where(
        lax.broadcasted_iota(jnp.int32, (groups, groups), 0)
        == lax.broadcasted_iota(jnp.int32, (groups, groups), 1),
        -decay_ref[...],
        0.0,
    )
    log_step = dot(eye, step_ref[...], (1, 0), HIGH)
    cum_ref[...] = dot(tri, log_step, (1, 1), HIGH)
    cumt_ref[...] = dot(log_step, tri, (1, 1), HIGH)
    row = lax.broadcasted_iota(jnp.int32, (rows, rows), 0)
    col = lax.broadcasted_iota(jnp.int32, (rows, rows), 1)
    steps[...] = dot(jnp.where(row == col, 1.0, 0.0), step_ref[...], (1, 1), HIGH)
    pad = jnp.zeros((16, 2 * size - groups), F32)
    total = jnp.concatenate(
        [jnp.broadcast_to(cum_ref[pl.ds(rows - 1, 1)], (16, groups)), pad], axis=1
    )
    line = lax.broadcasted_iota(jnp.int32, total.shape, 0)
    one = total.astype(BF16).astype(F32)
    two = (total - one).astype(BF16).astype(F32)
    kv[pl.ds(rows, 16)] = jnp.where(
        line == 0, one, jnp.where(line == 1, two, jnp.where(line == 2, total - one - two, 0.0))
    ).astype(BF16)
    seg = jnp.where(seg_ref[...] == 0, 1.0, 0.0)
    bound = jnp.sum(jnp.sum(seg, axis=1, keepdims=True), axis=0, keepdims=True)
    loads[0].wait()
    pl.semaphore_wait(barrier, len(peers))

    sent = []

    def cp(k, slot, to, part=None, own=False):
        dst = kvall.at[slot] if part is None else kvall.at[slot, part]
        from_kv = kv if part is None else kv.at[part]
        copy = remote(from_kv if own else dst, dst, ssem.at[k], rsem.at[k], (to, tp))
        copy.start()
        sent.append(copy)
        return copy

    def hp(k, slot, to, part=None):
        dst = hid.at[slot] if part is None else hid.at[slot, part]
        copy = remote(dst, dst, hssem.at[k], hrsem.at[k], (c, to))
        copy.start()
        sent.append(copy)
        return copy

    lo, hi = pl.ds(0, 128), pl.ds(128, kv.shape[0] - 128)
    z0 = [cp(0, me, zp, lo, own=True)]
    r0 = [cp(1, me, right, lo, own=True)]
    l0 = [cp(2, me, left, hi, own=True)]
    z0.append(cp(3, me, zp, hi, own=True))
    r0.append(cp(4, me, right, hi, own=True))
    l0.append(cp(5, me, left, lo, own=True))
    m0 = cp(6, me, mate, own=True)
    mine = pltpu.make_async_copy(kv, kvall.at[me], lsem.at[0])
    mine.start()
    hid_own.wait()
    h1 = hp(1, tme, tup)
    h2 = hp(2, tme, tdown)

    y_acc[:, : heads * size] = jnp.full((rows, heads * size), -jnp.inf, F32)
    local[...] = jnp.zeros_like(local)
    y_acc[:, heads * size :] = jnp.zeros((rows, heads * size), F32)
    p[...] = jnp.zeros_like(p)
    reach = 3 * 4096 // (4 * rows)
    first = jnp.maximum(me - reach, 0)
    for load in loads[1:]:
        load.wait()
    q_pos = (me * rows + row).astype(F32)
    floor = jnp.where(q_pos >= bound, bound, 0.0)

    def twice(a):
        return jnp.concatenate([a, a], axis=1)

    def scores(j):
        @pl.when((j <= me) & (j >= first))
        def _():
            k = kvall[j, :rows, :size]
            k_pos = (j * rows + col).astype(F32)
            bias = jnp.where((k_pos <= q_pos) & (k_pos >= floor), 0.0, -1e30)
            for h in range(heads):
                s = dot(q4[h], k, (1, 1)) + bias
                s_ref[j - first, h] = s
                y_acc[:, h * size : (h + 1) * size] = jnp.maximum(y_acc[:, h * size : (h + 1) * size], jnp.maximum(s[:, :size], s[:, size:]))

    def weigh(low, high, use_it, group):
        def step(j, _):
            @pl.when(use_it(j) & (j <= me) & (j >= first))
            def _():
                v = jnp.concatenate([kvall[j, :rows, size:], jnp.ones((rows, size), BF16)], axis=1)
                for h in range(heads):
                    e = jnp.exp((s_ref[j - first, h] - twice(top[group, h])) * scaling)
                    s_ref[j - first, h] = e
                    local[:, 2 * h * size : (2 * h + 2) * size] += dot(e.astype(BF16), v, (1, 0))

            return 0

        lax.fori_loop(low, high, step, 0)

    def raise_top(group):
        for h in range(heads):
            high = jnp.broadcast_to(jnp.max(y_acc[:, h * size : (h + 1) * size], axis=1, keepdims=True), (rows, size))
            if group > 0:
                local[:, 2 * h * size : (2 * h + 2) * size] = local[:, 2 * h * size : (2 * h + 2) * size] * twice(jnp.exp((top[group - 1, h] - high) * scaling))
            top[group, h] = high

    def always(j):
        return j >= 0

    mine.wait()
    scores(me)
    r0[0].wait_recv()
    f1 = cp(7, left, right, lo)
    l0[0].wait_recv()
    f2 = cp(8, right, left, hi)
    m0.wait_recv()
    scores(mate)
    z0[0].wait_recv()
    zr = [cp(9, zp, right, lo)]
    zl = [cp(10, zp, left, lo)]
    r0[1].wait_recv()
    m1 = cp(11, left, mate)
    l0[1].wait_recv()
    m2 = cp(12, right, mate)
    z0[1].wait_recv()
    zl.append(cp(13, zp, left, hi))
    zr.append(cp(14, zp, right, hi))
    m3 = cp(15, zp, mate)
    h0 = hp(0, tme, tzp)
    scores(left)
    f1.wait_recv()
    m4 = cp(16, opp, mate, lo)
    f2.wait_recv()
    m5 = cp(17, opp, mate, hi)
    scores(right)
    scores(opp)
    m1.wait_recv()
    scores(at(zh, x + 3, 1 - core))
    zright, zleft, zopp = at(1 - zh, x + 1, core), at(1 - zh, x + 3, core), at(1 - zh, x + 2, core)
    zr[0].wait_recv()
    f3 = cp(18, zleft, right, lo)
    m2.wait_recv()
    scores(at(zh, x + 1, 1 - core))
    m4.wait_recv()
    m5.wait_recv()
    scores(at(zh, x + 2, 1 - core))
    raise_top(0)
    zl[1].wait_recv()
    f4 = cp(19, zright, left, hi)
    zr[1].wait_recv()
    m6 = cp(20, zleft, mate)
    zl[0].wait_recv()
    m7 = cp(21, zright, mate)
    near_low = jnp.maximum(first, zh * 8)
    near_mid = (near_low + me + 1) // 2
    weigh(near_low, near_mid, always, 0)
    f3.wait_recv()
    m8 = cp(22, zopp, mate, lo)
    f4.wait_recv()
    m9 = cp(23, zopp, mate, hi)
    weigh(near_mid, me + 1, always, 0)
    h0.wait_recv()
    h1.wait_recv()
    h2.wait_recv()
    h5 = hp(5, tdown, tup, pl.ds(0, 128))
    h6 = hp(6, tup, tdown, pl.ds(128, 128))
    h3 = hp(3, tzp, tup)
    h4 = hp(4, tzp, tdown)
    scores(zp)
    scores(zleft)
    scores(zright)
    m3.wait_recv()
    scores(at(1 - zh, x, 1 - core))
    m6.wait_recv()
    scores(at(1 - zh, x + 3, 1 - core))
    m7.wait_recv()
    scores(at(1 - zh, x + 1, 1 - core))
    raise_top(1)
    far = lax.rem(x + 2, 4)
    away = (1 - zh) * 8
    weigh(away, away + 8, lambda j: lax.rem(j // 2, 4) != far, 1)
    scores(zopp)
    m8.wait_recv()
    m9.wait_recv()
    scores(at(1 - zh, x + 2, 1 - core))
    raise_top(2)
    weigh(away + 2 * far, away + 2 * far + 2, always, 2)

    logs[...] = (
        kvall[:, rows, :groups].astype(F32)
        + kvall[:, rows + 1, :groups].astype(F32)
        + kvall[:, rows + 2, :groups].astype(F32)
    )
    for h in range(heads):
        inverse = 1.0 / local[:, (2 * h + 1) * size : (2 * h + 2) * size]
        out = local[:, 2 * h * size : (2 * h + 1) * size] * inverse
        corr = jnp.sum(out * g4[h].astype(F32), axis=1, keepdims=True)
        y_acc[:, h * size : (h + 1) * size] = jnp.broadcast_to(corr, (rows, size))
        last = top[2, h]
        for group in range(3):
            top[group, h] = inverse * jnp.exp((top[group, h] - last) * scaling)

    h5.wait_recv()
    h7 = hp(7, topp, tzp, pl.ds(0, 128))
    h6.wait_recv()
    h8 = hp(8, topp, tzp, pl.ds(128, 128))

    def grads(d, c_at):
        def one_z(n, _):
            z = jnp.where(n == 0, 1 - zh, zh)
            group = jnp.where(n == 0, 2 if d == 2 else 1, 0)
            j = at(z, x + d, c_at)

            @pl.when((j <= me) & (j >= first))
            def _():
                k = kvall[j, :rows, :size]
                v = kvall[j, :rows, size:]
                for h in range(heads):
                    t = s_ref[j - first, h] * twice(top[group, h])
                    e = (t * (dot(g4[h], v, (1, 1)) - twice(y_acc[:, h * size : (h + 1) * size]))).astype(BF16)
                    t4[h] = t.astype(BF16)
                    d4[h] = e
                    y_acc[:, (heads + h) * size : (heads + h + 1) * size] += dot(e, k, (1, 0))
                dk = dot(d4[...].reshape(heads * rows, rows), q4[...].reshape(heads * rows, size), (0, 0))
                dv = dot(t4[...].reshape(heads * rows, rows), g4[...].reshape(heads * rows, size), (0, 0))
                p[z, lax.rem(x + d, 4), c_at] = jnp.concatenate([dk * scaling, dv], axis=1).astype(BF16)

            return 0

        lax.fori_loop(0, 2, one_z, 0)

    half = rows // 2
    low, high = pl.ds(0, half), pl.ds(half, half)

    def sp(k, src, dst, to):
        copy = remote(src, dst, ssem.at[24 + k], rsem.at[24 + k], (to, tp))
        copy.start()
        sent.append(copy)
        return copy

    def to_mate(k, d):
        grads(d, 1 - core)
        return sp(k, p.at[:, lax.rem(x + d, 4), 1 - core], got.at[d], mate)

    def both(d, z):
        return p[z, lax.rem(x + d, 4), core].astype(F32) + got[d, z].astype(F32)

    order = (1 - zh, zh)
    g2 = to_mate(0, 2)
    grads(2, core)
    g2.wait_recv()
    t0, t1, u0, u1 = [], [], [], []
    for n, z in enumerate(order):
        tout[z] = both(2, z).astype(BF16)
        t0.append(sp(4 + n, tout.at[z, low], uin.at[0, z], right))
        t1.append(sp(6 + n, tout.at[z, high], uin.at[1, z], left))
    g1 = to_mate(1, 1)
    grads(1, core)
    g3 = to_mate(2, 3)
    grads(3, core)
    g1.wait_recv()
    g3.wait_recv()
    for n, z in enumerate(order):
        u = both(1, z)
        uout[0, z, high] = u[half:].astype(BF16)
        t0[n].wait_recv()
        uout[0, z, low] = (u[:half] + uin[0, z].astype(F32)).astype(BF16)
        u0.append(sp(8 + n, uout.at[0, z], vin.at[0, z], right))
        u = both(3, z)
        uout[1, z, low] = u[:half].astype(BF16)
        t1[n].wait_recv()
        uout[1, z, high] = (u[half:] + uin[1, z].astype(F32)).astype(BF16)
        u1.append(sp(10 + n, uout.at[1, z], vin.at[1, z], left))
    g0 = to_mate(3, 0)
    grads(0, core)
    for h in range(heads):
        dq_ref[:, h * size : (h + 1) * size] = (y_acc[:, (heads + h) * size : (heads + h + 1) * size] * scaling).astype(BF16)
    g0.wait_recv()

    def whole(n, z):
        u0[n].wait_recv()
        u1[n].wait_recv()
        return (
            p[z, x, core].astype(F32)
            + got[0, z].astype(F32)
            + vin[0, z].astype(F32)
            + vin[1, z].astype(F32)
        )

    zout[...] = whole(0, 1 - zh).astype(BF16)
    zc = sp(12, zout, zin, zp)
    kept = whole(1, zh)
    zc.wait_recv()
    kvg_ref[...] = (kept + zin[...].astype(F32)).astype(BF16)
    h3.wait_recv()
    h4.wait_recv()
    h7.wait_recv()
    h8.wait_recv()
    for copy in sent:
        copy.wait_send()

    width = up_ref.shape[1]
    inner = mixed.shape[1]
    state_size = inner // groups

    def part(k):
        return pl.ds(pl.multiple_of(k * width, width), width)

    for index, value in enumerate(prefix_weights(logs[...], groups)):
        w_ref[index] = value
    weights[0].wait()
    weights[1].wait()
    for load in more:
        load.wait()

    def attn_term(k):
        return dot(dq_ref[...], qw[part(k)], (1, 1)) + dot(kvg_ref[...], kw[part(k)], (1, 1))

    def mix():
        weights[3].wait()

        def step(k, _):
            y_acc[...] += dot(hid[k], mw[part(k)], (1, 0))
            return 0

        y_acc[...] = jnp.zeros_like(y_acc)
        lax.fori_loop(0, 8, step, 0)
        mixed[...] = y_acc[...].astype(BF16)

    mid = sent_sums(
        attn_term, lambda: up_ref[...].astype(F32), (tin, tuin, rin, rv, rout), 0, tssem, trsem, mix
    ).astype(BF16)
    mid_ref[...] = mid
    weights[2].wait()
    y_acc[...] = jnp.zeros_like(y_acc)

    def out_term(k):
        y_acc[...] += dot(everyone[k], ow[:, part(k)], (1, 1))

    spread_out(mid, everyone, 14, tssem, trsem, out_term)
    y[...] = y_acc[...].astype(BF16)

    spot = lax.broadcasted_iota(jnp.int32, (groups, inner), 1)
    head = lax.broadcasted_iota(jnp.int32, (groups, inner), 0) * state_size
    wide = jnp.where((spot >= head) & (spot < head + state_size), 1.0, 0.0).astype(BF16)

    def widen(value):
        high = value.astype(BF16)
        low = (value - high.astype(F32)).astype(BF16)
        return dot(high, wide, (1, 0)) + dot(low, wide, (1, 0))

    cum = cum_ref[...]
    weighted = (y[...].astype(F32) * widen(jnp.exp(cum))).astype(BF16)
    terms[...] = dot(weighted, c_ref[...], (0, 0)).reshape(terms.shape)
    count = groups // 2
    begin = core * count
    half = count // 2
    theirs_at = pl.ds((1 - core) * count, count)
    ours = pl.ds(begin, count)
    copies = []

    def pp(k, src, dst, to):
        copy = remote(src, dst, tssem.at[28 + k], trsem.at[28 + k], (to, tp))
        copy.start()
        copies.append(copy)
        return copy

    ours_out[...] = terms[...].astype(BF16)
    a_heads, b_heads = pl.ds(0, half), pl.ds(half, half)
    away_at = (1 - core) * count
    c0 = [
        pp(n, ours_out.at[pl.ds(away_at + n * half, half)], theirs.at[pl.ds(away_at + n * half, half)], mate)
        for n in range(2)
    ]
    c1 = pp(2, ours_out.at[ours], theirs.at[ours], mate)

    def w(k, h):
        return w_ref[k, pl.ds(begin + h, 1), :]

    inner_bc = dot(b_ref[...], c_ref[...], (1, 1))
    later = col >= row
    left_lane = lax.broadcasted_iota(jnp.int32, (rows, 2 * state_size), 1) < state_size

    def decay(h):
        spread = cumt_ref[pl.ds(h, 1), :] - cum_ref[:, h : h + 1]
        return jnp.exp(jnp.where(later, spread, -1e30))

    def pair_of(ref, p):
        both = ref[:, p * 2 * state_size : (p + 1) * 2 * state_size]
        none = jnp.zeros_like(both)
        return jnp.where(left_lane, both, none), jnp.where(left_lane, none, both), both

    def local_pairs(start, stop):
        for p in range(start, stop):
            y0, y1, _ = pair_of(y, p)
            a0 = (inner_bc * decay(2 * p)).astype(BF16)
            a1 = (inner_bc * decay(2 * p + 1)).astype(BF16)
            local[:, p * 2 * state_size : (p + 1) * 2 * state_size] = dot(a0, y0, (1, 0)) + dot(a1, y1, (1, 0))

    def chip_terms(n):
        c0[n].wait_recv()
        for h in range(n * half, (n + 1) * half):
            gx[0, h] = (
                w(0, h) * terms[begin + h] + w(1, h) * theirs[begin + h].astype(F32)
            ).astype(BF16)

    chip_terms(0)
    r0a = pp(3, gx.at[0, a_heads], gx.at[3, a_heads], right)
    chip_terms(1)
    l0b = pp(4, gx.at[0, b_heads], gx.at[1, b_heads], left)
    l0a = pp(5, gx.at[0, a_heads], gx.at[1, a_heads], left)
    r0b = pp(6, gx.at[0, b_heads], gx.at[3, b_heads], right)
    local_pairs(0, 2)
    r0a.wait_recv()
    r1 = pp(7, gx.at[3, a_heads], gx.at[2, a_heads], right)
    l0b.wait_recv()
    l1 = pp(8, gx.at[1, b_heads], gx.at[2, b_heads], left)
    local_pairs(2, 5)

    def weigh_states(base, h):
        return sum(w(base + d, h) * gx[d, h].astype(F32) for d in range(4))

    l0a.wait_recv()
    r1.wait_recv()
    for h in range(half):
        hout[h] = weigh_states(2, h).astype(BF16)
    z0a = pp(9, hout.at[a_heads], hin.at[a_heads], zp)
    r0b.wait_recv()
    l1.wait_recv()
    for h in range(half, count):
        hout[h] = weigh_states(2, h).astype(BF16)
    z0b = pp(10, hout.at[b_heads], hin.at[b_heads], zp)
    local_pairs(5, 8)
    e0 = []
    for n, (z_n, part_n) in enumerate(((z0a, a_heads), (z0b, b_heads))):
        z_n.wait_recv()
        for h in range(n * half, (n + 1) * half):
            eout[h] = (weigh_states(6, h) + w(10, h) * hin[h].astype(F32)).astype(BF16)
        e0.append(pp(11 + n, eout.at[part_n], ein.at[part_n], mate))
    c1.wait_recv()

    def finish(start, e):
        for h in range(count):
            at_h = pl.ds(start + h, 1)
            carried[start + h] = (
                w_ref[12, at_h, :] * theirs[start + h].astype(F32)
                + w_ref[11, at_h, :] * e[h].astype(F32)
            ).astype(BF16)

    finish(begin, eout)
    ending = widen(jnp.exp(cum_ref[pl.ds(rows - 1, 1)] - cum))
    stepping = widen(steps[...])
    skipping = widen(jnp.broadcast_to(skip_ref[...], (rows, groups)))
    for copy in e0:
        copy.wait_recv()
    finish((1 - core) * count, ein)
    state = carried[...].reshape(inner, terms.shape[2])
    y_float = y[...].astype(F32)
    grad_in = (
        stepping * (local[...] + dot(b_ref[...], state, (1, 1)) * ending) + skipping * y_float
    ).astype(BF16)
    y_acc[...] = stepping * ending

    def mix_term(k):
        return dot(grad_in, mw[part(k)], (1, 1))

    def states():
        scaled = (mixed[...].astype(F32) * y_acc[...]).astype(BF16)
        s_ref[0, 0] = jnp.zeros((rows, rows), F32)
        for p in range(groups // 2):
            m0, m1, _ = pair_of(mixed, p)
            both = y[:, p * 2 * state_size : (p + 1) * 2 * state_size]
            for h, m in ((2 * p, m0), (2 * p + 1, m1)):
                s_ref[0, 0] += dot(m, both, (1, 1)) * decay(h) * steps[:, h : h + 1]
        state_ref[...] = dot(s_ref[0, 0].astype(BF16), c_ref[...], (1, 0)) + dot(
            scaled, state, (1, 0)
        )

    hidden_ref[...] = sent_sums(
        mix_term, lambda: mid_ref[...].astype(F32), (tin, tuin, rin, rv, rout), 42, tssem, trsem, states
    ).astype(BF16)
    for copy in copies:
        copy.wait_send()


def whole(arrays, cid):
    keyval, query, _, hidden, qw, kw, ow, mw, upstream, b, c, step = arrays[:12]
    rows, cols = keyval.shape
    size = cols // 2
    heads = query.shape[1] // size
    groups = step.shape[0]
    inner = mw.shape[1]
    full = upstream.shape
    state = (groups, inner // groups, b.shape[1])
    part = (groups // 2,) + state[1:]
    any_spec = pl.BlockSpec(memory_space=pl.ANY)
    two = (2, rows, cols)
    vm = pltpu.VMEM
    dma = pltpu.SemaphoreType.DMA
    return pl.pallas_call(
        whole_kernel,
        out_shape=(
            jax.ShapeDtypeStruct(full, BF16),
            jax.ShapeDtypeStruct(full, BF16),
            jax.ShapeDtypeStruct((rows, b.shape[1]), F32),
        ),
        in_specs=[any_spec] * 11 + [VM] * 4,
        out_specs=(VM,) * 3,
        scratch_shapes=[
            vm((rows + 16, cols), BF16),
            vm((16, rows + 16, cols), BF16),
            vm((13, heads, rows, rows), F32),
            vm((heads, rows, size), BF16),
            vm((heads, rows, size), BF16),
            vm((3, heads, rows, size), F32),
            vm((heads, rows, rows), BF16),
            vm((heads, rows, rows), BF16),
            vm((2, 4, 2, rows, cols), BF16),
            vm((4,) + two, BF16),
            vm((2, 2, rows // 2, cols), BF16),
            vm((2,) + two, BF16),
            vm((rows, cols), BF16),
            vm(two, BF16),
            vm((2,) + two, BF16),
            vm((rows, cols), BF16),
            vm(query.shape, BF16),
            vm(keyval.shape, BF16),
            vm((8,) + hidden.shape, BF16),
            vm((rows, groups), F32),
            vm((groups, rows), F32),
            vm((rows, groups), F32),
            vm((16, groups), F32),
            vm(qw.shape, BF16),
            vm(kw.shape, BF16),
            vm(ow.shape, BF16),
            vm(mw.shape, BF16),
            vm(full, BF16),
            vm(b.shape, BF16),
            vm(c.shape, BF16),
            vm(full, BF16),
            vm((2, rows // 2, full[1]), BF16),
            vm((4,) + full, BF16),
            vm(full, BF16),
            vm((7,) + full, BF16),
            vm((8,) + full, BF16),
            vm((rows, inner), F32),
            vm((rows, inner), BF16),
            vm((rows, inner), BF16),
            vm((rows, inner), F32),
            vm((13, groups, 128), F32),
            vm(state, F32),
            vm(state, BF16),
            vm(state, BF16),
            vm((4,) + part, BF16),
            vm(part, BF16),
            vm(part, BF16),
            vm(part, BF16),
            vm(part, BF16),
            vm(state, BF16),
            dma((37,)),
            dma((37,)),
            dma((9,)),
            dma((9,)),
            dma((56,)),
            dma((56,)),
            dma((17,)),
        ],
        compiler_params=pltpu.CompilerParams(
            collective_id=cid, has_side_effects=True, vmem_limit_bytes=(64 << 20) - (256 << 10)
        ),
        name="whole",
    )(*arrays)


def finish_kernel(a_ref, b_ref, c_ref, a_out, b_out, c_out):
    a_out[...] = a_ref[...]
    b_out[...] = b_ref[...]
    c_out[...] = c_ref[...]


def finish(arrays):
    return pl.pallas_call(
        finish_kernel,
        out_shape=tuple(jax.ShapeDtypeStruct(a.shape, a.dtype) for a in arrays),
        in_specs=[VM] * 3,
        out_specs=(VM,) * 3,
        name="finish",
    )(*arrays)


def on_device(
    hidden_in,
    upstream,
    query_ckpt,
    keyval_ckpt,
    attn_out_grad,
    segments,
    query_weight,
    keyval_weight,
    mix_weight,
    out_weight,
    state_in_ckpt,
    state_out_ckpt,
    step_size,
    decay_rate,
    skip_gain,
):
    return finish(
        whole(
            (
                keyval_ckpt,
                query_ckpt,
                attn_out_grad,
                hidden_in,
                query_weight,
                keyval_weight,
                out_weight,
                mix_weight,
                upstream,
                state_in_ckpt,
                state_out_ckpt,
                step_size.T,
                decay_rate[None, :],
                segments.reshape(-1, 128),
                skip_gain[None, :],
            ),
            1,
        )
    )


def solution(mesh):
    placed = (
        P("ctx", "tp"),
        P("ctx", "tp"),
        P("ctx", "tp"),
        P("ctx", "tp"),
        P("ctx", "tp"),
        P(),
        P(None, "tp"),
        P(None, "tp"),
        P(None, "tp"),
        P("tp", None),
        P("ctx", "tp"),
        P("ctx", "tp"),
        P("ctx", "tp"),
        P("tp"),
        P("tp"),
    )
    return jax.shard_map(
        on_device,
        mesh=mesh,
        in_specs=placed,
        out_specs=(P("ctx", "tp"), P("ctx", "tp"), P("ctx", "tp")),
        check_vma=False,
    )
```

profile of v0, /device:TPU:8, one launch (start us, length us, event | category | flops | bytes accessed | tf_op | source)
XLA Modules:
  0.0 121.5 jit_solution(2686985992087566352)
XLA Ops:
  0.6 119.0 %whole.1 = (bf16[256,512]{1,0:T(8,128)(2,1)}, bf16[256,512]{1,0:T(8,128)(2,1)}, f32[256,128]{1,0:T(8,128)}) custom-call(bf16[256,256]{1,0:T(8,128)(2,1)} %kv_hbm.1, bf16[256,512]{1,0:T(8,128)(2,1)} %q_hbm.1, bf16[256,512]{1,0:T(8,128)(2,1)} %g_hbm.1, bf16[256,512]{1,0:T(8,128)(2,1)} %hid_hbm.1, bf16[4096,512]{1,0:T(8,128)(2,1)} %qw_hbm.1, ...), custom_call_target="tpu_custom_call" | custom-call | tf_op jit(solution)/shard_map/whole/pallas_call | solution.py:760
  119.6 1.9 %finish.1 = (bf16[256,512]{1,0:T(8,128)(2,1)}, bf16[256,512]{1,0:T(8,128)(2,1)}, f32[256,128]{1,0:T(8,128)}) custom-call(bf16[256,512]{1,0:T(8,128)(2,1)} %get-tuple-element.6.a_ref, bf16[256,512]{1,0:T(8,128)(2,1)} %get-tuple-element.7.b_ref, f32[256,128]{1,0:T(8,128)} %get-tuple-element.8.c_ref), custom_call_target="tpu_custom_call" | custom-call | tf_op jit(solution)/shard_map/finish/pallas_call | solution.py:842
where the time goes:
time: 123 us; the launch traced here: 122 us
  Pallas kernels  121 us (98%)
    pallas_call x1, Pallas kernels, whole(): pl.pallas_call(whole_kernel, out_shape=(jax.ShapeDtypeStruct(full, BF16),...  119 us

commit v1 on v0

--- a/solution.py
+++ b/solution.py
@@ -220,7 +220,7 @@
     kv_hbm, q_hbm, g_hbm, hid_hbm, qw_hbm, kw_hbm, ow_hbm, mw_hbm, up_hbm, b_hbm, c_hbm,
     step_ref, decay_ref, seg_ref, skip_ref,
     mid_ref, hidden_ref, state_ref,
-    kv, kvall, s_ref, q4, g4, top, t4, d4, p,
+    kv, kvall, s_ref, q4, g4, stat, top, t4, d4, p,
     got, uin, vin, zin, tout, uout, zout, dq_ref, kvg_ref, hid, cum_ref, cumt_ref, steps, logs,
     qw, kw, ow, mw, up_ref, b_ref, c_ref, tin, tuin, rin, rv, rout, everyone, y_acc, y, mixed,
     local, w_ref, terms, ours_out, theirs, gx, hout, hin, eout, ein, carried,
@@ -318,40 +318,43 @@
     h1 = hp(1, tme, tup)
     h2 = hp(2, tme, tdown)
 
-    y_acc[:, : heads * size] = jnp.full((rows, heads * size), -jnp.inf, F32)
+    stat[...] = jnp.full_like(stat, -jnp.inf)
     local[...] = jnp.zeros_like(local)
-    y_acc[:, heads * size :] = jnp.zeros((rows, heads * size), F32)
+    y_acc[...] = jnp.zeros_like(y_acc)
     p[...] = jnp.zeros_like(p)
     reach = 3 * 4096 // (4 * rows)
     first = jnp.maximum(me - reach, 0)
     for load in loads[1:]:
         load.wait()
-    q_pos = (me * rows + row).astype(F32)
+    q_pos = (me * rows + col).astype(F32)
     floor = jnp.where(q_pos >= bound, bound, 0.0)
 
-    def twice(a):
-        return jnp.concatenate([a, a], axis=1)
+    tall = size + 16
+
+    def lanes_of(h):
+        return slice(h * rows, (h + 1) * rows)
 
     def scores(j):
         @pl.when((j <= me) & (j >= first))
         def _():
             k = kvall[j, :rows, :size]
-            k_pos = (j * rows + col).astype(F32)
+            k_pos = (j * rows + row).astype(F32)
             bias = jnp.where((k_pos <= q_pos) & (k_pos >= floor), 0.0, -1e30)
             for h in range(heads):
-                s = dot(q4[h], k, (1, 1)) + bias
+                s = dot(k, q4[h], (1, 1)) + bias
                 s_ref[j - first, h] = s
-                y_acc[:, h * size : (h + 1) * size] = jnp.maximum(y_acc[:, h * size : (h + 1) * size], jnp.maximum(s[:, :size], s[:, size:]))
+                stat[h] = jnp.maximum(stat[h], jnp.max(s.reshape(rows // 8, 8, rows), axis=0))
 
     def weigh(low, high, use_it, group):
         def step(j, _):
             @pl.when(use_it(j) & (j <= me) & (j >= first))
             def _():
-                v = jnp.concatenate([kvall[j, :rows, size:], jnp.ones((rows, size), BF16)], axis=1)
+                v = kvall[j, :rows, size:].astype(F32).T.astype(BF16)
+                v = jnp.concatenate([v, jnp.ones((16, rows), BF16)], axis=0)
                 for h in range(heads):
-                    e = jnp.exp((s_ref[j - first, h] - twice(top[group, h])) * scaling)
+                    e = jnp.exp((s_ref[j - first, h] - top[group, h, 0:1, :]) * scaling)
                     s_ref[j - first, h] = e
-                    local[:, 2 * h * size : (2 * h + 2) * size] += dot(e.astype(BF16), v, (1, 0))
+                    local[:tall, lanes_of(h)] += dot(v, e.astype(BF16), (1, 0))
 
             return 0
 
@@ -359,10 +362,12 @@
 
     def raise_top(group):
         for h in range(heads):
-            high = jnp.broadcast_to(jnp.max(y_acc[:, h * size : (h + 1) * size], axis=1, keepdims=True), (rows, size))
+            high = jnp.max(stat[h], axis=0, keepdims=True)
             if group > 0:
-                local[:, 2 * h * size : (2 * h + 2) * size] = local[:, 2 * h * size : (2 * h + 2) * size] * twice(jnp.exp((top[group - 1, h] - high) * scaling))
-            top[group, h] = high
+                local[:tall, lanes_of(h)] = local[:tall, lanes_of(h)] * jnp.exp(
+                    (top[group - 1, h, 0:1, :] - high) * scaling
+                )
+            top[group, h] = jnp.broadcast_to(high, (8, rows))
 
     def always(j):
         return j >= 0
@@ -452,10 +457,10 @@
         + kvall[:, rows + 2, :groups].astype(F32)
     )
     for h in range(heads):
-        inverse = 1.0 / local[:, (2 * h + 1) * size : (2 * h + 2) * size]
-        out = local[:, 2 * h * size : (2 * h + 1) * size] * inverse
-        corr = jnp.sum(out * g4[h].astype(F32), axis=1, keepdims=True)
-        y_acc[:, h * size : (h + 1) * size] = jnp.broadcast_to(corr, (rows, size))
+        inverse = 1.0 / local[size : size + 1, lanes_of(h)]
+        out = local[:size, lanes_of(h)] * inverse
+        corr = jnp.sum(out * g4[h].astype(F32).T, axis=0, keepdims=True)
+        stat[h] = jnp.broadcast_to(corr, (8, rows))
         last = top[2, h]
         for group in range(3):
             top[group, h] = inverse * jnp.exp((top[group, h] - last) * scaling)
@@ -476,13 +481,13 @@
                 k = kvall[j, :rows, :size]
                 v = kvall[j, :rows, size:]
                 for h in range(heads):
-                    t = s_ref[j - first, h] * twice(top[group, h])
-                    e = (t * (dot(g4[h], v, (1, 1)) - twice(y_acc[:, h * size : (h + 1) * size]))).astype(BF16)
-                    t4[h] = t.astype(BF16)
-                    d4[h] = e
-                    y_acc[:, (heads + h) * size : (heads + h + 1) * size] += dot(e, k, (1, 0))
-                dk = dot(d4[...].reshape(heads * rows, rows), q4[...].reshape(heads * rows, size), (0, 0))
-                dv = dot(t4[...].reshape(heads * rows, rows), g4[...].reshape(heads * rows, size), (0, 0))
+                    t = s_ref[j - first, h] * top[group, h, 0:1, :]
+                    e = t * (dot(v, g4[h], (1, 1)) - stat[h, 0:1, :])
+                    t4[:, lanes_of(h)] = t.astype(BF16)
+                    d4[:, lanes_of(h)] = e.astype(BF16)
+                y_acc[:size] += dot(k.astype(F32).T.astype(BF16), d4[...], (1, 0))
+                dk = dot(d4[...], q4[...].reshape(heads * rows, size), (1, 0))
+                dv = dot(t4[...], g4[...].reshape(heads * rows, size), (1, 0))
                 p[z, lax.rem(x + d, 4), c_at] = jnp.concatenate([dk * scaling, dv], axis=1).astype(BF16)
 
             return 0
@@ -534,7 +539,7 @@
     g0 = to_mate(3, 0)
     grads(0, core)
     for h in range(heads):
-        dq_ref[:, h * size : (h + 1) * size] = (y_acc[:, (heads + h) * size : (heads + h + 1) * size] * scaling).astype(BF16)
+        dq_ref[:, h * size : (h + 1) * size] = (y_acc[:size, lanes_of(h)].T * scaling).astype(BF16)
     g0.wait_recv()
 
     def whole(n, z):
@@ -576,7 +581,17 @@
     def attn_term(k):
         return dot(dq_ref[...], qw[part(k)], (1, 1)) + dot(kvg_ref[...], kw[part(k)], (1, 1))
 
+    spot = lax.broadcasted_iota(jnp.int32, (groups, inner), 1)
+    head = lax.broadcasted_iota(jnp.int32, (groups, inner), 0) * state_size
+    wide = jnp.where((spot >= head) & (spot < head + state_size), 1.0, 0.0).astype(BF16)
+
+    def widen(value):
+        high = value.astype(BF16)
+        low = (value - high.astype(F32)).astype(BF16)
+        return dot(high, wide, (1, 0)) + dot(low, wide, (1, 0))
+
     def mix():
+        local[...] = widen(jnp.exp(cum_ref[...]))
         weights[3].wait()
 
         def step(k, _):
@@ -600,18 +615,7 @@
     spread_out(mid, everyone, 14, tssem, trsem, out_term)
     y[...] = y_acc[...].astype(BF16)
 
-    spot = lax.broadcasted_iota(jnp.int32, (groups, inner), 1)
-    head = lax.broadcasted_iota(jnp.int32, (groups, inner), 0) * state_size
-    wide = jnp.where((spot >= head) & (spot < head + state_size), 1.0, 0.0).astype(BF16)
-
-    def widen(value):
-        high = value.astype(BF16)
-        low = (value - high.astype(F32)).astype(BF16)
-        return dot(high, wide, (1, 0)) + dot(low, wide, (1, 0))
-
     cum = cum_ref[...]
-    weighted = (y[...].astype(F32) * widen(jnp.exp(cum))).astype(BF16)
-    terms[...] = dot(weighted, c_ref[...], (0, 0)).reshape(terms.shape)
     count = groups // 2
     begin = core * count
     half = count // 2
@@ -625,13 +629,23 @@
         copies.append(copy)
         return copy
 
-    ours_out[...] = terms[...].astype(BF16)
+    wide_half = inner // 2
+
+    def state_terms(c_at):
+        lanes = pl.ds(pl.multiple_of(c_at * wide_half, wide_half), wide_half)
+        weighted = (y[:, lanes].astype(F32) * local[:, lanes]).astype(BF16)
+        found = dot(weighted, c_ref[...], (0, 0)).reshape((count,) + terms.shape[1:])
+        terms[pl.ds(c_at * count, count)] = found
+        ours_out[pl.ds(c_at * count, count)] = found.astype(BF16)
+
+    state_terms(1 - core)
     a_heads, b_heads = pl.ds(0, half), pl.ds(half, half)
     away_at = (1 - core) * count
     c0 = [
         pp(n, ours_out.at[pl.ds(away_at + n * half, half)], theirs.at[pl.ds(away_at + n * half, half)], mate)
         for n in range(2)
     ]
+    state_terms(core)
     c1 = pp(2, ours_out.at[ours], theirs.at[ours], mate)
 
     def w(k, h):
@@ -691,6 +705,11 @@
         hout[h] = weigh_states(2, h).astype(BF16)
     z0b = pp(10, hout.at[b_heads], hin.at[b_heads], zp)
     local_pairs(5, 8)
+    stepping = widen(steps[...])
+    y_acc[...] = stepping * widen(jnp.exp(cum_ref[pl.ds(rows - 1, 1)] - cum))
+    local[...] = stepping * local[...] + widen(
+        jnp.broadcast_to(skip_ref[...], (rows, groups))
+    ) * y[...].astype(F32)
     e0 = []
     for n, (z_n, part_n) in enumerate(((z0a, a_heads), (z0b, b_heads))):
         z_n.wait_recv()
@@ -708,18 +727,11 @@
             ).astype(BF16)
 
     finish(begin, eout)
-    ending = widen(jnp.exp(cum_ref[pl.ds(rows - 1, 1)] - cum))
-    stepping = widen(steps[...])
-    skipping = widen(jnp.broadcast_to(skip_ref[...], (rows, groups)))
     for copy in e0:
         copy.wait_recv()
     finish((1 - core) * count, ein)
     state = carried[...].reshape(inner, terms.shape[2])
-    y_float = y[...].astype(F32)
-    grad_in = (
-        stepping * (local[...] + dot(b_ref[...], state, (1, 1)) * ending) + skipping * y_float
-    ).astype(BF16)
-    y_acc[...] = stepping * ending
+    grad_in = (local[...] + dot(b_ref[...], state, (1, 1)) * y_acc[...]).astype(BF16)
 
     def mix_term(k):
         return dot(grad_in, mw[part(k)], (1, 1))
@@ -772,9 +784,10 @@
             vm((13, heads, rows, rows), F32),
             vm((heads, rows, size), BF16),
             vm((heads, rows, size), BF16),
-            vm((3, heads, rows, size), F32),
-            vm((heads, rows, rows), BF16),
-            vm((heads, rows, rows), BF16),
+            vm((heads, 8, rows), F32),
+            vm((3, heads, 8, rows), F32),
+            vm((rows, heads * rows), BF16),
+            vm((rows, heads * rows), BF16),
             vm((2, 4, 2, rows, cols), BF16),
             vm((4,) + two, BF16),
             vm((2, 2, rows // 2, cols), BF16),

time: 123 us -> 121 us (0.984)
  Pallas kernels: 121 us -> 119 us
    pallas_call x1, Pallas kernels: 119 us -> 118 us  [whole(): pl.pallas_call(whole_kernel, out_shape=(jax.ShapeDtypeStruct(full, BF16),...]
where the time goes in v1:
time: 121 us; the launch traced here: 120 us
  Pallas kernels  119 us (98%)
    pallas_call x1, Pallas kernels, whole(): pl.pallas_call(whole_kernel, out_shape=(jax.ShapeDtypeStruct(full, BF16),...  118 us

profile of v1, /device:TPU:8, one launch (start us, length us, event | category | flops | bytes accessed | tf_op | source)
XLA Modules:
  0.0 120.1 jit_solution(4013271905773578901)
XLA Ops:
  0.6 117.6 %whole.1 = (bf16[256,512]{1,0:T(8,128)(2,1)}, bf16[256,512]{1,0:T(8,128)(2,1)}, f32[256,128]{1,0:T(8,128)}) custom-call(bf16[256,256]{1,0:T(8,128)(2,1)} %kv_hbm.1, bf16[256,512]{1,0:T(8,128)(2,1)} %q_hbm.1, bf16[256,512]{1,0:T(8,128)(2,1)} %g_hbm.1, bf16[256,512]{1,0:T(8,128)(2,1)} %hid_hbm.1, bf16[4096,512]{1,0:T(8,128)(2,1)} %qw_hbm.1, ...), custom_call_target="tpu_custom_call" | custom-call | tf_op jit(solution)/shard_map/whole/pallas_call | solution.py:772
  118.2 1.9 %finish.1 = (bf16[256,512]{1,0:T(8,128)(2,1)}, bf16[256,512]{1,0:T(8,128)(2,1)}, f32[256,128]{1,0:T(8,128)}) custom-call(bf16[256,512]{1,0:T(8,128)(2,1)} %get-tuple-element.6.a_ref, bf16[256,512]{1,0:T(8,128)(2,1)} %get-tuple-element.7.b_ref, f32[256,128]{1,0:T(8,128)} %get-tuple-element.8.c_ref), custom_call_target="tpu_custom_call" | custom-call | tf_op jit(solution)/shard_map/finish/pallas_call | solution.py:855
